TPU v7x, 1024 devices: a whole 4x4x32 slice. The times are simulated.
1024 devices in a mesh: expert: 16 (over y, x_lo, core), dp: 64 (over x_hi, z).
Axes of the slice: x: 4 (x_hi: 2, x_lo: 2; x = x_hi * 2 + x_lo), y: 4, z: 32, core: 2. Of those that a mesh axis runs over, the one named last changes fastest.
Arguments:
- tokens: bfloat16 [8192, 2048], P('dp'), may hold values from -6 to 6
- cotangent: bfloat16 [8192, 2048], P('dp'), may hold values from -6 to 6
- gate_values: float32 [8192, 2], P('dp'), may hold values from 0.2 to 1
- expert_ids: int32 [8192, 2], P('dp'), may hold values from 0 to 63, all different within a row
- weight_in: bfloat16 [64, 2048, 4096], P('dp', None, 'expert'), may hold values from -0.125 to 0.125
- weight_out: bfloat16 [64, 4096, 2048], P('dp', 'expert'), may hold values from -0.09375 to 0.09375
Outputs:
- input_grad: bfloat16 [8192, 2048], P('dp', 'expert')
- weight_out_grad: bfloat16 [64, 4096, 2048], P('dp', 'expert')
All inputs are finite; a program needn't handle non-finite values.
Results may differ from a plain program's by a relative error of at most 0.0057.
Values may be sent and summed in bfloat16 or wider, within the bound.
A program may use at most 32 MiB of HBM per device.

v0:
```python
import jax
import jax.numpy as jnp
from jax import lax
from jax.sharding import PartitionSpec as P

CAP = 4


def shards(tokens, cotangent, gate_values, expert_ids, weight_in, weight_out):
    groups = lax.axis_size("dp")
    per_device = weight_in.shape[0]
    model_width = tokens.shape[1]
    per_group = tokens.shape[0]
    expert_count = groups * per_device
    slot_total = expert_count * CAP
    flattened = expert_ids.reshape(-1)
    onehot = (flattened[:, None] == jnp.arange(expert_count, dtype=jnp.int32)[None, :]).astype(
        jnp.int32
    )
    before = jnp.cumsum(onehot, axis=0) - onehot
    position = jnp.sum(before * onehot, axis=1)
    target = jnp.where(position < CAP, flattened * CAP + position, -1).reshape(per_group, 2)
    slot_table = target[:, :, None] == jnp.arange(slot_total, dtype=jnp.int32)[None, None, :]
    dispatch = jnp.any(slot_table, axis=1)
    dispatch_half = dispatch.astype(jnp.bfloat16)
    dispatch_full = dispatch.astype(jnp.float32)
    slot_gate = jnp.sum(slot_table.astype(jnp.float32) * gate_values[:, :, None], axis=(0, 1))
    sent_tokens = jnp.dot(dispatch_half.T, tokens, preferred_element_type=jnp.float32).astype(
        jnp.bfloat16
    )
    sent_grads = (
        jnp.dot(dispatch_half.T, cotangent, preferred_element_type=jnp.float32) * slot_gate[:, None]
    ).astype(jnp.bfloat16)
    sent_tokens = sent_tokens.reshape(groups, per_device * CAP, model_width)
    sent_grads = sent_grads.reshape(groups, per_device * CAP, model_width)
    got_tokens, got_grads = (
        lax.all_to_all(sent_tokens, "dp", split_axis=0, concat_axis=0, tiled=True),
        lax.all_to_all(sent_grads, "dp", split_axis=0, concat_axis=0, tiled=True),
    )
    slot_tokens = got_tokens.reshape(groups, per_device, CAP, model_width)
    slot_grads = got_grads.reshape(groups, per_device, CAP, model_width)
    preact = jnp.einsum(
        "sjcd,jdf->sjcf", slot_tokens, weight_in, preferred_element_type=jnp.float32
    )
    hidden, puller = jax.vjp(jax.nn.gelu, preact)
    post_grad = jnp.einsum(
        "sjcd,jfd->sjcf", slot_grads, weight_out, preferred_element_type=jnp.float32
    )
    pre_grad = puller(post_grad)[0].astype(jnp.bfloat16)
    weight_out_grad = jnp.einsum(
        "sjcf,sjcd->jfd",
        hidden.astype(jnp.bfloat16),
        slot_grads,
        preferred_element_type=jnp.float32,
    ).astype(jnp.bfloat16)
    kept_rows = model_width // lax.axis_size("expert")
    produced = jnp.einsum("jdf,sjcf->dsjc", weight_in, pre_grad, preferred_element_type=jnp.float32)
    column_terms = lax.psum_scatter(
        produced.reshape(kept_rows * lax.axis_size("expert"), slot_total),
        "expert",
        scatter_dimension=0,
        tiled=True,
    )
    returned = lax.all_to_all(column_terms, "dp", split_axis=1, concat_axis=1, tiled=True)
    summed = jnp.einsum("ds,ts->td", returned, dispatch_full, precision=lax.Precision.HIGHEST)
    input_grad = summed.astype(jnp.bfloat16)
    return (input_grad, weight_out_grad)


def solution(mesh):
    placed = (
        P("dp", None),
        P("dp", None),
        P("dp", None),
        P("dp", None),
        P("dp", None, "expert"),
        P("dp", "expert", None),
    )
    return jax.shard_map(
        shards,
        mesh=mesh,
        in_specs=placed,
        out_specs=(P("dp", "expert"), P("dp", "expert", None)),
        check_vma=False,
    )
```

profile of v0, /device:TPU:27, one launch (start us, length us, event | category | flops | bytes accessed | tf_op | source)
XLA Modules:
  0.0 406.1 jit_solution(11313252744219319249)
XLA Ops:
  7.2 0.0 copy-start
  7.2 0.8 broadcast_multiply_fusion
  7.9 0.8 copy.31
  8.7 0.1 eq.42
  8.9 0.1 eq.38
  9.0 0.1 copy.35
  9.1 0.6 reduce-window.6
  9.8 0.2 slice_reduce_fusion
  10.0 0.1 fusion.45
  10.1 0.1 reduce_sum.21
  10.3 0.1 copy.36
  10.3 0.1 fusion.29
  10.5 1.5 convolution_convert_fusion
  12.0 0.0 copy-start.3
  12.0 1.2 reshape.73
  13.2 30.6 %all-to-all-start.1 = ((bf16[64,4,2048]{2,1,0:T(4,128)(2,1)}), bf16[64,4,2048]{2,1,0:T(4,128)(2,1)S(1)}, u32[]{:S(2)}, u32[]{:S(2)}) async-start(bf16[64,4,2048]{2,1,0:T(4,128)(2,1)} %reshape.73), calls=%async_computation.1 | async-start | bytes 2097152 | tf_op jit(solution)/shard_map/all_to_all | solution.py:37
  43.8 0.0 copy-done.3
  43.9 0.1 select_reduce_fusion
  44.0 1.5 fusion
  45.5 1.2 reshape.71
  46.8 89.3 %all-to-all-done.1 = bf16[64,4,2048]{2,1,0:T(4,128)(2,1)S(1)} async-done(((bf16[64,4,2048]{2,1,0:T(4,128)(2,1)}), bf16[64,4,2048]{2,1,0:T(4,128)(2,1)S(1)}, u32[]{:S(2)}, u32[]{:S(2)}) %all-to-all-start.1) | async-done | bytes 1048608 | tf_op jit(solution)/shard_map/all_to_all | solution.py:37
  136.0 23.1 %all-to-all-start = ((bf16[64,4,2048]{2,1,0:T(4,128)(2,1)}), bf16[64,4,2048]{2,1,0:T(4,128)(2,1)S(1)}, u32[]{:S(2)}, u32[]{:S(2)}) async-start(bf16[64,4,2048]{2,1,0:T(4,128)(2,1)} %reshape.71), calls=%async_computation | async-start | bytes 2097152 | tf_op jit(solution)/shard_map/all_to_all | solution.py:38
  159.2 0.0 reduce-scatter.2.cloned.1.call-start
  159.2 0.0 copy-done
  159.2 1.3 convolution_bitcast_fusion.2
  160.5 90.6 %all-to-all-done = bf16[64,4,2048]{2,1,0:T(4,128)(2,1)S(1)} async-done(((bf16[64,4,2048]{2,1,0:T(4,128)(2,1)}), bf16[64,4,2048]{2,1,0:T(4,128)(2,1)S(1)}, u32[]{:S(2)}, u32[]{:S(2)}) %all-to-all-start) | async-done | bytes 1048608 | tf_op jit(solution)/shard_map/all_to_all | solution.py:38
  251.0 0.0 copy-start.1
  251.1 1.0 copy-done.1
  252.0 4.1 %convolution_bitcast_fusion.1 = f32[2048,64,1,4]{0,1,3,2:T(8,128)} fusion(bf16[1,2048,256]{2,1,0:T(8,128)(2,1)S(1)} %copy-done, f32[64,1,4,256]{3,0,2,1:T(8,128)S(1)} %convolution_bitcast_fusion.2, bf16[1,256,2048]{2,1,0:T(8,128)(2,1)} %param.11, bf16[64,4,2048]{2,1,0:T(4,128)(2,1)S(1)} %all-to-all-done), kind=kOutput, calls=%fused_computation.1 | convolution fusion | flops 538181632 | bytes 5505024 | tf_op jit(solution)/shard_map/jdf,sjcf->dsjc/dot_general | solution.py:57
  256.1 2.9 copy.39
  259.0 1.8 reshape.76
  260.8 0.0 copy-start.2
  260.8 0.0 reduce-scatter.2.cloned.1.call-update
  260.8 82.4 %reduce-scatter.2.cloned.1.call-done = f32[128,256]{0,1:T(8,128)} async-done(((f32[2048,256]{0,1:T(8,128)}), f32[128,256]{0,1:T(8,128)}) %reduce-scatter.2.cloned.1.call-update) | async-done | bytes 131088 | tf_op jit(solution)/shard_map/reduce_scatter | solution.py:58
  343.2 22.7 %all-to-all-start.2 = ((f32[128,64,4]{0,2,1:T(4,128)}), f32[128,64,4]{0,2,1:T(4,128)S(1)}, u32[]{:S(2)}, u32[]{:S(2)}) async-start(f32[128,64,4]{0,2,1:T(4,128)} %bitcast.83), calls=%async_computation.3 | async-start | bytes 262144 | tf_op jit(solution)/shard_map/all_to_all | solution.py:64
  365.9 0.0 copy-done.2
  365.9 2.4 fusion.2
  368.3 30.0 %all-to-all-done.2 = f32[128,64,4]{0,2,1:T(4,128)S(1)} async-done(((f32[128,64,4]{0,2,1:T(4,128)}), f32[128,64,4]{0,2,1:T(4,128)S(1)}, u32[]{:S(2)}, u32[]{:S(2)}) %all-to-all-start.2) | async-done | bytes 131104 | tf_op jit(solution)/shard_map/all_to_all | solution.py:64
  398.4 0.8 convolution_convert_fusion.1
  (4 shorter events, 0.1 us)
Async XLA Ops:
  7.2 152.0 %copy-start = (bf16[1,2048,256]{2,1,0:T(8,128)(2,1)S(1)}, bf16[1,2048,256]{2,1,0:T(8,128)(2,1)}, u32[]{:S(2)}) copy-start(bf16[1,2048,256]{2,1,0:T(8,128)(2,1)} %param.10) | copy-start | bytes 3145732
  12.0 31.9 %copy-start.3 = (f32[128,2]{0,1:T(2,128)S(1)}, f32[128,2]{0,1:T(2,128)}, u32[]{:S(2)}) copy-start(f32[128,2]{0,1:T(2,128)} %param.8) | copy-start | bytes 3076
  13.2 122.8 %all-to-all-start.1 = ((bf16[64,4,2048]{2,1,0:T(4,128)(2,1)}), bf16[64,4,2048]{2,1,0:T(4,128)(2,1)S(1)}, u32[]{:S(2)}, u32[]{:S(2)}) async-start(bf16[64,4,2048]{2,1,0:T(4,128)(2,1)} %reshape.73), calls=%async_computation.1 | async-start | bytes 2097152 | tf_op jit(solution)/shard_map/all_to_all | solution.py:37
  136.0 115.0 %all-to-all-start = ((bf16[64,4,2048]{2,1,0:T(4,128)(2,1)}), bf16[64,4,2048]{2,1,0:T(4,128)(2,1)S(1)}, u32[]{:S(2)}, u32[]{:S(2)}) async-start(bf16[64,4,2048]{2,1,0:T(4,128)(2,1)} %reshape.71), calls=%async_computation | async-start | bytes 2097152 | tf_op jit(solution)/shard_map/all_to_all | solution.py:38
  159.2 184.0 %reduce-scatter.2.cloned.1.call-start = ((), (), s32[]{:S(2)}) async-start(), calls=%async_computation.4 | async-start | bytes 2228224 | tf_op jit(solution)/shard_map/reduce_scatter | solution.py:58
  251.0 1.0 copy-start.1
  260.8 105.1 %copy-start.2 = (bf16[64,4,2048]{2,1,0:T(4,128)(2,1)S(1)}, bf16[64,4,2048]{2,1,0:T(4,128)(2,1)}, u32[]{:S(2)}) copy-start(bf16[64,4,2048]{2,1,0:T(4,128)(2,1)} %copy-done.1) | copy-start | bytes 3145732
  343.2 55.2 %all-to-all-start.2 = ((f32[128,64,4]{0,2,1:T(4,128)}), f32[128,64,4]{0,2,1:T(4,128)S(1)}, u32[]{:S(2)}, u32[]{:S(2)}) async-start(f32[128,64,4]{0,2,1:T(4,128)} %bitcast.83), calls=%async_computation.3 | async-start | bytes 262144 | tf_op jit(solution)/shard_map/all_to_all | solution.py:64
Sparse Core Ops, SparseCore 0:
  261.0 82.1 reduce-scatter.1
where the time goes:
time: 407 us; the launch traced here: 406 us
  waiting for transfers between devices  292 us (72%)
  starting transfers between devices  76.5 us (19%)
  between operations  14.2 us (3%)
  matrix products  11.6 us (3%)
  local copies, waits for them, and re-layouts  9.72 us (2%)
    all_to_all x1, waiting for transfers between devices, shards(): lax.all_to_all(sent_grads, 'dp', split_axis=0, concat_axis=0, tiled=True)  90.6 us
    all_to_all x1, waiting for transfers between devices, shards(): lax.all_to_all(sent_tokens, 'dp', split_axis=0, concat_axis=0, tiled=True)  89.3 us
    reduce_scatter x1, waiting for transfers between devices, shards(): lax.psum_scatter(produced.reshape(kept_rows * lax.axis_size('expert'), sl...  82.4 us
    all_to_all x1, starting transfers between devices, shards(): lax.all_to_all(sent_tokens, 'dp', split_axis=0, concat_axis=0, tiled=True)  30.6 us
    all_to_all x1, waiting for transfers between devices, shards(): lax.all_to_all(column_terms, 'dp', split_axis=1, concat_axis=1, tiled=True)  30 us
    all_to_all x1, starting transfers between devices, shards(): lax.all_to_all(sent_grads, 'dp', split_axis=0, concat_axis=0, tiled=True)  23.1 us
    all_to_all x1, starting transfers between devices, shards(): lax.all_to_all(column_terms, 'dp', split_axis=1, concat_axis=1, tiled=True)  22.7 us
  transfers between devices with their start and end apart: 4, of which 4 were waited for; matrix products, arithmetic and copies ran while one was open for 2% of the time, Pallas kernels for 0%

commit v1 on v0

v1 whole, which is shorter than its diff:
```python
import functools

import jax
import jax.numpy as jnp
from jax import lax
from jax.experimental import pallas as pl
from jax.experimental.pallas import tpu as pltpu
from jax.sharding import PartitionSpec as P

CAP = 4
PLANE = 16
NZ = 32
WAYS = 4
ROWS = WAYS * CAP
F32 = jnp.float32
BF16 = jnp.bfloat16
NT = (((1,), (1,)), ((), ()))
TN = (((0,), (0,)), ((), ()))
K0 = 0.7978845608028654
K1 = 0.044715


def rem(a, b):
    return lax.rem(a, b)


def iota(shape, dim):
    return lax.broadcasted_iota(jnp.int32, shape, dim)


def offsets(a):
    return (a + 1, 16 - a, 32 - a, 17 + a)


def kernel(
    tok_hbm, cot_hbm, ids_ref, gate_ref, win_hbm, wout_hbm, out_ref, wog_hbm,
    tok, cot, win, wout, wog, tx, rx, rows_all, pre_grad, hid,
    e1s, e1r, q_ref, e2s, e2r, e3s, e3r, e4s, e4r, fs, fr, ts, tr, dall,
    ld_sem, b_s, b_r, c1_s, c1_r, c2_s, c2_r, c3_s, c3_r, sib_s, sib_r,
    e1_ss, e1_rs, e2_ss, e2_rs, e3_ss, e3_rs, e4_ss, e4_rs, f_ss, f_rs, t_ss, t_rs,
):
    width = tok.shape[1]
    m = lax.axis_index("expert")
    d = lax.axis_index("dp")
    y, xl, c = m // 4, rem(m // 2, 2), rem(m, 2)
    xh, z = d // NZ, rem(d, NZ)
    a = y * 2 + xl
    p = c * 8 + a
    off = offsets(a)
    xo = rem(xh + c, 2)
    dest = [xo * NZ + rem(z + o, NZ) for o in off]
    source = [xo * NZ + rem(z + NZ - o, NZ) for o in off]
    to_self = (a == 0) & (c == 0)
    sibling = m + 1 - 2 * c
    partner = m + 2 - 4 * xl
    up = rem(y + 1, 4) * 4 + rem(m, 4)
    down = rem(y + 3, 4) * 4 + rem(m, 4)

    def plane_index(q):
        return rem(q, 8) * 2 + q // 8

    loads = [
        pltpu.make_async_copy(src, dst, ld_sem.at[i])
        for i, (src, dst) in enumerate(((tok_hbm, tok), (cot_hbm, cot), (win_hbm, win), (wout_hbm, wout)))
    ]
    for copy in loads:
        copy.start()
    barrier = pltpu.get_barrier_semaphore()

    def greet(e, dp):
        pl.semaphore_signal(barrier, inc=1, device_id={"expert": e, "dp": dp}, device_id_type=pl.DeviceIdType.MESH)

    for j in range(WAYS):
        if j == 2:
            @pl.when(jnp.logical_not(to_self))
            def _():
                greet(m, dest[2])
                greet(m, source[2])
        else:
            greet(m, dest[j])
            greet(m, source[j])
    for i in range(1, PLANE):
        greet(plane_index(rem(p + i, PLANE)), d)

    id0, id1 = ids_ref[0:1, :], ids_ref[1:2, :]
    g0, g1 = gate_ref[0:1, :], gate_ref[1:2, :]
    count = id0.shape[1]
    earlier = (iota((count, count), 0) < iota((count, count), 1)).astype(BF16)

    def slots(expert, slot):
        one0, one1 = id0 == expert, id1 == expert
        one = one0 | one1
        before = jnp.dot(one.astype(F32).astype(BF16), earlier, preferred_element_type=F32)
        taken = one & (before.astype(jnp.int32) == slot)
        return taken, one0

    r = iota((4 * ROWS, 1), 0)
    rj, rq, rs = r // 16, rem(r // 4, 4), rem(r, 4)
    expert = jnp.where(rj == 0, dest[0], jnp.where(rj == 1, dest[1], jnp.where(rj == 2, dest[2], dest[3])))
    taken, one0 = slots(expert, rs)
    gate = jnp.sum(jnp.where(taken, jnp.where(one0, g0, g1), 0.0), axis=1, keepdims=True)
    picks = [(taken & (rq == q)).astype(F32).astype(BF16) for q in range(4)]
    quarter = width // 4

    def fill(stream, ref, scale):
        total = None
        for q in range(4):
            part = jnp.dot(picks[q], ref[:, q * quarter:(q + 1) * quarter], preferred_element_type=F32)
            total = part if total is None else total + part
        if scale is not None:
            total = total * scale
        tx[stream] = total.astype(BF16)

    loads[0].wait()
    fill(0, tok, None)
    pl.semaphore_wait(barrier, 8 + PLANE - 1 - 2 * to_self.astype(jnp.int32))

    waits = []

    def remote(src, dst, send, recv, e=None, dp=None):
        return pltpu.make_async_remote_copy(
            src_ref=src, dst_ref=dst, send_sem=send, recv_sem=recv,
            device_id={"expert": m if e is None else e, "dp": d if dp is None else dp},
            device_id_type=pl.DeviceIdType.MESH,
        )

    def go(copy):
        copy.start()
        waits.append(copy)
        return copy

    def exchange(src, dst, send, recv, dp, is_self):
        copy = remote(src, dst, send, recv, dp=dp)
        if not is_self:
            return go(copy)

        @pl.when(jnp.logical_not(to_self))
        def _():
            copy.start()

        @pl.when(to_self)
        def _():
            pltpu.make_async_copy(src, dst, recv).start()

        return copy

    guarded = []

    def block(ref, j):
        return ref.at[pl.ds(j * 16, 16)]

    def send_b(stream):
        out = []
        for j in (1, 3, 0, 2):
            copy = exchange(block(tx.at[stream], j), block(rx.at[stream], j), b_s.at[stream, j], b_r.at[stream, j], dest[j], j == 2)
            out.append(copy)
            if j == 2:
                guarded.append(copy)
        return out

    b_copies = [send_b(0)]
    loads[1].wait()
    fill(1, cot, gate)
    b_copies.append(send_b(1))

    t = iota((64, 64), 0)
    u = iota((64, 64), 1)
    swap = ((t // 16 == rem(u // 4, 4)) & (rem(t // 4, 4) == u // 16) & (rem(t, 4) == rem(u, 4))).astype(F32).astype(BF16)

    ar = iota((PLANE * ROWS, 1), 0)
    ap, aj, asl = ar // 16, rem(ar // 4, 4), rem(ar, 4)
    ac, aa = ap // 8, rem(ap, 8)
    aoff = jnp.where(aj == 0, aa + 1, jnp.where(aj == 1, 16 - aa, jnp.where(aj == 2, 32 - aa, 17 + aa)))
    aexpert = rem(xh + ac, 2) * NZ + rem(z + aoff, NZ)
    all_taken, _ = slots(aexpert, asl)
    dall[...] = all_taken.astype(F32).astype(BF16)

    def unpack(stream):
        for copy in b_copies[stream]:
            copy.wait_recv()
        got = jnp.dot(swap, rx[stream], preferred_element_type=F32).astype(BF16)
        for q in range(4):
            rows_all[stream, pl.ds(pl.multiple_of(p * 16, 16), 16), q * quarter:(q + 1) * quarter] = got[q * 16:(q + 1) * 16]

    def part(stream, row, size):
        return rows_all.at[stream, pl.ds(pl.multiple_of(row, 16), size)]

    sibs = [[], []]

    def to_sibling(stream, row, size):
        k = len(sibs[stream])
        ref = part(stream, row, size)
        sibs[stream].append(go(remote(ref, ref, sib_s.at[stream, k], sib_r.at[stream, k], e=sibling)))

    base = c * 128
    y_up, y_down, y_far = rem(y + 1, 4), rem(y + 3, 4), rem(y + 2, 4)

    def gather_1(stream):
        ref = part(stream, p * 16, 16)
        copy = go(remote(ref, ref, c1_s.at[stream], c1_r.at[stream], e=partner))
        to_sibling(stream, p * 16, 16)
        return copy

    def gather_2(stream, first):
        first.wait_recv()
        ref = part(stream, base + y * 32, 32)
        copies = [
            go(remote(ref, ref, c2_s.at[stream, 0], c2_r.at[stream, 0], e=up)),
            go(remote(ref, ref, c2_s.at[stream, 1], c2_r.at[stream, 1], e=down)),
        ]
        to_sibling(stream, base + y * 32 + (1 - xl) * 16, 16)
        return copies

    def gather_3(stream, second):
        second[0].wait_recv()
        low = part(stream, base + y_down * 32, 16)
        copies = [go(remote(low, low, c3_s.at[stream, 0], c3_r.at[stream, 0], e=up))]
        second[1].wait_recv()
        high = part(stream, base + y_up * 32 + 16, 16)
        copies.append(go(remote(high, high, c3_s.at[stream, 1], c3_r.at[stream, 1], e=down)))
        to_sibling(stream, base + y_down * 32, 32)
        to_sibling(stream, base + y_up * 32, 32)
        return copies

    def gather_4(stream, third):
        for copy in third:
            copy.wait_recv()
        to_sibling(stream, base + y_far * 32, 32)

    unpack(0)
    first_x = gather_1(0)
    second_x = gather_2(0, first_x)
    third_x = gather_3(0, second_x)
    unpack(1)
    first_g = gather_1(1)
    gather_4(0, third_x)
    second_g = gather_2(1, first_g)
    for copy in sibs[0]:
        copy.wait_recv()
    loads[2].wait()
    preact = jnp.zeros((256, win.shape[1]), F32)
    for k in range(4):
        cols = slice(k * quarter, (k + 1) * quarter)
        preact = preact + jnp.dot(rows_all[0, :, cols], win[cols, :], preferred_element_type=F32)
    third_g = gather_3(1, second_g)
    square = preact * preact
    th = jnp.tanh(K0 * preact * (1.0 + K1 * square))
    hid[...] = (0.5 * preact * (1.0 + th)).astype(BF16)
    slope = 0.5 * (1.0 + th) + 0.5 * preact * (1.0 - th * th) * (K0 * (1.0 + 3.0 * K1 * square))
    gather_4(1, third_g)
    for copy in sibs[1]:
        copy.wait_recv()
    loads[3].wait()
    post = jnp.zeros((256, wout.shape[0]), F32)
    for k in range(4):
        cols = slice(k * quarter, (k + 1) * quarter)
        post = post + lax.dot_general(rows_all[1, :, cols], wout[:, cols], NT, preferred_element_type=F32)
    pre_grad[...] = (post * slope).astype(BF16)

    half = width // 2
    e1 = []
    for h in range(2):
        theirs = pre_grad[pl.ds(pl.multiple_of((1 - c) * 128, 128), 128), :]
        for k in range(2):
            cols = slice(h * half + k * quarter, h * half + (k + 1) * quarter)
            e1s[h, :, k * quarter:(k + 1) * quarter] = lax.dot_general(
                theirs, win[cols, :], NT, preferred_element_type=F32).astype(BF16)
        e1.append(go(remote(e1s.at[h], e1r.at[h], e1_ss.at[h], e1_rs.at[h], e=sibling)))
    for h in range(2):
        ours = pre_grad[pl.ds(pl.multiple_of(c * 128, 128), 128), :]
        for k in range(2):
            cols = slice(h * half + k * quarter, h * half + (k + 1) * quarter)
            q_ref[h, :, k * quarter:(k + 1) * quarter] = lax.dot_general(
                ours, win[cols, :], NT, preferred_element_type=F32)

    def q_rows(h, row, size):
        return q_ref[h, pl.ds(pl.multiple_of(row, 16), size), :]

    e2, e3 = [], []
    for h in range(2):
        e1[h].wait_recv()
        q_ref[h] = q_ref[h] + e1r[h].astype(F32)
        for k, target in enumerate((up, down)):
            e2s[h, k] = q_rows(h, y_far * 32 + k * 16, 16).astype(BF16)
            e2.append(go(remote(e2s.at[h, k], e2r.at[h, k], e2_ss.at[h, k], e2_rs.at[h, k], e=target)))
        for k, (target, yt) in enumerate(((up, y_up), (down, y_down))):
            other = 1 - k
            e3s[h, k, other] = q_rows(h, yt * 32 + other * 16, 16).astype(BF16)
            e3.append(go(remote(e3s.at[h, k, other], e3r.at[h, k, other], e3_ss.at[h, k, other], e3_rs.at[h, k, other], e=target)))
    for h in range(2):
        for k, (target, yt) in enumerate(((up, y_up), (down, y_down))):
            e2[2 * h + k].wait_recv()
            e3s[h, k, k] = (q_rows(h, yt * 32 + k * 16, 16) + e2r[h, k].astype(F32)).astype(BF16)
            e3.append(go(remote(e3s.at[h, k, k], e3r.at[h, k, k], e3_ss.at[h, k, k], e3_rs.at[h, k, k], e=target)))

    turned = hid[...].astype(F32).T.astype(BF16)
    for k in range(4):
        cols = slice(k * quarter, (k + 1) * quarter)
        wog[:, cols] = jnp.dot(turned, rows_all[1, :, cols], preferred_element_type=F32).astype(BF16)
    store = pltpu.make_async_copy(wog, wog_hbm, ld_sem.at[4])
    store.start()

    e4 = []
    for h in range(2):
        for copy in (e3[2 * h], e3[2 * h + 1], e3[4 + 2 * h], e3[5 + 2 * h]):
            copy.wait_recv()
        total = q_rows(h, y * 32, 32)
        for k in range(2):
            total = total + jnp.concatenate([e3r[h, k, 0], e3r[h, k, 1]], axis=0).astype(F32)
        q_ref[h, pl.ds(pl.multiple_of(y * 32, 32), 32), :] = total
        e4s[h] = q_rows(h, y * 32 + (1 - xl) * 16, 16).astype(BF16)
        e4.append(go(remote(e4s.at[h], e4r.at[h], e4_ss.at[h], e4_rs.at[h], e=partner)))

    eighth = width // 8
    f_copies = []
    for h in range(2):
        e4[h].wait_recv()
        total = (q_rows(h, y * 32 + xl * 16, 16) + e4r[h].astype(F32)).astype(BF16)
        stacked = jnp.concatenate([total[:, q * eighth:(q + 1) * eighth] for q in range(4)], axis=0)
        fs[h] = jnp.dot(swap, stacked, preferred_element_type=F32).astype(BF16)
        row = []
        for j in (1, 3, 0, 2):
            copy = exchange(block(fs.at[h], j), block(fr.at[h], j), f_ss.at[h, j], f_rs.at[h, j], source[j], j == 2)
            row.append(copy)
            if j == 2:
                guarded.append(copy)
        f_copies.append(row)

    t_copies = []
    for h in range(2):
        for copy in f_copies[h]:
            copy.wait_recv()
        got = jnp.dot(swap, fr[h], preferred_element_type=F32).astype(BF16)
        for k in range(8):
            ts[h * 8 + k] = got[(k // 2) * 16:(k // 2 + 1) * 16, (k % 2) * 128:(k % 2 + 1) * 128]
        for k in range(8):
            target = h * 8 + rem(k + m, 8)
            src, dst = ts.at[target], tr.at[pl.ds(pl.multiple_of(p * 16, 16), 16)]
            copy = remote(src, dst, t_ss.at[target], t_rs.at[p], e=target)

            @pl.when(target != m)
            def _():
                copy.start()

            @pl.when(target == m)
            def _():
                pltpu.make_async_copy(src, dst, t_rs.at[p]).start()

            t_copies.append((target, copy))

    for q in range(PLANE):
        remote(ts.at[0], tr.at[pl.ds(q * 16, 16)], t_ss.at[0], t_rs.at[q]).wait_recv()
    out_ref[...] = lax.dot_general(dall[...], tr[...], TN, preferred_element_type=F32).astype(BF16)

    for copy in waits:
        copy.wait_send()

    @pl.when(jnp.logical_not(to_self))
    def _():
        for copy in guarded:
            copy.wait_send()

    for target, copy in t_copies:
        @pl.when(target != m)
        def _():
            copy.wait_send()
    store.wait()


def shards(tokens, cotangent, gate_values, expert_ids, weight_in, weight_out):
    count, width = tokens.shape
    hidden = weight_in.shape[2]
    dma = pltpu.SemaphoreType.DMA
    half = width // 2
    vmem = pl.BlockSpec(memory_space=pltpu.VMEM)
    hbm = pl.BlockSpec(memory_space=pl.ANY)
    rows = PLANE * ROWS
    out, grad = pl.pallas_call(
        kernel,
        out_shape=(
            jax.ShapeDtypeStruct((count, width // PLANE), BF16),
            jax.ShapeDtypeStruct((hidden, width), BF16),
        ),
        in_specs=[hbm, hbm, vmem, vmem, hbm, hbm],
        out_specs=(vmem, hbm),
        scratch_shapes=[
            pltpu.VMEM((count, width), BF16),
            pltpu.VMEM((count, width), BF16),
            pltpu.VMEM((width, hidden), BF16),
            pltpu.VMEM((hidden, width), BF16),
            pltpu.VMEM((hidden, width), BF16),
            pltpu.VMEM((2, 64, width // 4), BF16),
            pltpu.VMEM((2, 64, width // 4), BF16),
            pltpu.VMEM((2, rows, width), BF16),
            pltpu.VMEM((rows, hidden), BF16),
            pltpu.VMEM((rows, hidden), BF16),
            pltpu.VMEM((2, rows // 2, half), BF16),
            pltpu.VMEM((2, rows // 2, half), BF16),
            pltpu.VMEM((2, rows // 2, half), F32),
            pltpu.VMEM((2, 2, 16, half), BF16),
            pltpu.VMEM((2, 2, 16, half), BF16),
            pltpu.VMEM((2, 2, 2, 16, half), BF16),
            pltpu.VMEM((2, 2, 2, 16, half), BF16),
            pltpu.VMEM((2, 16, half), BF16),
            pltpu.VMEM((2, 16, half), BF16),
            pltpu.VMEM((2, 64, half // 4), BF16),
            pltpu.VMEM((2, 64, half // 4), BF16),
            pltpu.VMEM((PLANE, 16, width // PLANE), BF16),
            pltpu.VMEM((rows, width // PLANE), BF16),
            pltpu.VMEM((rows, count), BF16),
            dma((5,)),
            dma((2, 4)), dma((2, 4)),
            dma((2,)), dma((2,)),
            dma((2, 2)), dma((2, 2)),
            dma((2, 2)), dma((2, 2)),
            dma((2, 5)), dma((2, 5)),
            dma((2,)), dma((2,)),
            dma((2, 2)), dma((2, 2)),
            dma((2, 2, 2)), dma((2, 2, 2)),
            dma((2,)), dma((2,)),
            dma((2, 4)), dma((2, 4)),
            dma((PLANE,)), dma((PLANE,)),
        ],
        compiler_params=pltpu.CompilerParams(
            collective_id=0, has_side_effects=True, vmem_limit_bytes=40 * 1024 * 1024
        ),
    )(tokens, cotangent, expert_ids.T, gate_values.T, weight_in[0], weight_out[0])
    return out, grad[None]


def solution(mesh):
    placed = (
        P("dp", None),
        P("dp", None),
        P("dp", None),
        P("dp", None),
        P("dp", None, "expert"),
        P("dp", "expert", None),
    )
    return jax.shard_map(
        shards,
        mesh=mesh,
        in_specs=placed,
        out_specs=(P("dp", "expert"), P("dp", "expert", None)),
        check_vma=False,
    )
```

time: 407 us -> 110 us (0.27)
  the two profiles are of different devices: /device:TPU:27 before, /device:TPU:7 now
where the time goes in v1:
time: 110 us; the launch traced here: 109 us
  Pallas kernels  102 us (93%)
  local copies, waits for them, and re-layouts  6.8 us (6%)
    pallas_call x1, Pallas kernels, shards(): pl.pallas_call(kernel, out_shape=(jax.ShapeDtypeStruct((count, width // P...  102 us
    unnamed x14, local copies, waits for them, and re-layouts  6.8 us

profile of v1, /device:TPU:7, one launch (start us, length us, event | category | flops | bytes accessed | tf_op | source)
XLA Modules:
  0.0 109.0 jit_solution(6135980077596864617)
XLA Ops:
  0.6 0.0 copy-start.5
  0.6 0.0 copy-start.4
  0.7 0.7 copy-done.5
  1.3 0.0 copy-done.4
  1.3 0.0 copy-start
  1.3 1.2 %copy-done = bf16[1,2048,256]{2,1,0:T(8,128)(2,1)S(1)} copy-done((bf16[1,2048,256]{2,1,0:T(8,128)(2,1)S(1)}, bf16[1,2048,256]{2,1,0:T(8,128)(2,1)}, u32[]{:S(2)}) %copy-start) | copy-done | bytes 1048600
  2.6 0.0 copy-start.1
  2.6 1.2 %copy-done.1 = bf16[1,256,2048]{2,1,0:T(8,128)(2,1)S(1)} copy-done((bf16[1,256,2048]{2,1,0:T(8,128)(2,1)S(1)}, bf16[1,256,2048]{2,1,0:T(8,128)(2,1)}, u32[]{:S(2)}) %copy-start.1) | copy-done | bytes 1048600
  3.8 0.0 copy-start.2
  3.8 1.0 copy-done.2
  4.8 0.0 copy-start.3
  4.8 1.0 copy-done.3
  5.9 101.5 %shard_map.77 = (bf16[128,128]{1,0:T(8,128)(2,1)S(1)}, bf16[256,2048]{1,0:T(8,128)(2,1)S(1)}) custom-call(bf16[128,2048]{1,0:T(8,128)(2,1)S(1)} %copy-done.2, bf16[128,2048]{1,0:T(8,128)(2,1)S(1)} %copy-done.3, s32[2,128]{1,0:T(2,128)S(1)} %bitcast.8, f32[2,128]{1,0:T(2,128)S(1)} %bitcast.9, bf16[2048,256]{1,0:T(8,128)(2,1)S(1)} %bitcast.6, ...), custom_call_target="tpu_custom_call" | custom-call | tf_op jit(solution)/shard_map/pallas_call | solution.py:378
  107.4 0.6 copy.10
  108.0 1.0 copy.11
Async XLA Ops:
  0.6 0.7 copy-start.5
  0.6 0.7 copy-start.4
  1.3 1.2 %copy-start = (bf16[1,2048,256]{2,1,0:T(8,128)(2,1)S(1)}, bf16[1,2048,256]{2,1,0:T(8,128)(2,1)}, u32[]{:S(2)}) copy-start(bf16[1,2048,256]{2,1,0:T(8,128)(2,1)} %param.10) | copy-start | bytes 3145732
  2.6 1.2 %copy-start.1 = (bf16[1,256,2048]{2,1,0:T(8,128)(2,1)S(1)}, bf16[1,256,2048]{2,1,0:T(8,128)(2,1)}, u32[]{:S(2)}) copy-start(bf16[1,256,2048]{2,1,0:T(8,128)(2,1)} %param.11) | copy-start | bytes 3145732
  3.8 1.0 copy-start.2
  4.8 1.0 copy-start.3

commit v2 on v0

v2 whole, which is shorter than its diff:
```python
import functools

import jax
import jax.numpy as jnp
from jax import lax
from jax.experimental import pallas as pl
from jax.experimental.pallas import tpu as pltpu
from jax.sharding import PartitionSpec as P

CAP = 4
PLANE = 16
NZ = 32
F32 = jnp.float32
BF16 = jnp.bfloat16
NT = (((1,), (1,)), ((), ()))
TN = (((0,), (0,)), ((), ()))
K0 = 0.7978845608028654
K1 = 0.044715


def rem(a, b):
    return lax.rem(a, b)


def iota(shape, dim):
    return lax.broadcasted_iota(jnp.int32, shape, dim)


def offsets(s):
    return (s + 1, 32 - s, 8 - s, 25 + s, 16 - s, 17 + s, 9 + s, 24 - s)


def kernel(
    tok_hbm, cot_hbm, ids_ref, gate_ref, win_hbm, wout_hbm, out_ref, wog_hbm,
    tok, cot, win, wout, wog, tx, packed, x_ref, g_ref, g_sib, hid, hid_sib,
    es, er, q_ref, fs, fr, ts, tr, dall,
    ld_sem, b_s, b_r, w_s, w_r, ag_s, ag_r, g_ss, g_rs, h_ss, h_rs, e_ss, e_rs, f_ss, f_rs, t_ss, t_rs,
):
    half = tok.shape[1]
    piece = half // 4
    m = lax.axis_index("expert")
    d = lax.axis_index("dp")
    y, xl, c = m // 4, rem(m // 2, 2), rem(m, 2)
    xh, z = d // NZ, rem(d, NZ)
    s, fh = rem(y, 2) * 2 + xl, y // 2
    mine = rem(m, 8)
    off = offsets(s)
    xo = rem(xh + c, 2)
    dest = [xo * NZ + rem(z + o, NZ) for o in off]
    source = [xo * NZ + rem(z + NZ - o, NZ) for o in off]
    to_self = (s == 0) & (c == 0)
    sibling = m + 1 - 2 * c
    steps = [(dy, dx) for dy in (2, 1, 3, 0) for dx in (1, 0) if (dy, dx) != (0, 0)]

    def chip(dy, dx):
        ty, tx_ = rem(y + dy, 4), rem(xl + dx, 2)
        return rem(ty, 2) * 2 + tx_, ty // 2, ty * 4 + tx_ * 2 + c

    columns = pl.ds(pl.multiple_of(fh * half, 128), half)
    loads = [
        pltpu.make_async_copy(src, dst, ld_sem.at[i])
        for i, (src, dst) in enumerate(
            ((tok_hbm.at[:, columns], tok), (cot_hbm.at[:, columns], cot), (win_hbm, win.at[0]), (wout_hbm, wout.at[0])))
    ]
    for copy in loads:
        copy.start()
    barrier = pltpu.get_barrier_semaphore()

    def greet(e, dp):
        pl.semaphore_signal(barrier, inc=1, device_id={"expert": e, "dp": dp}, device_id_type=pl.DeviceIdType.MESH)

    order = (4, 5, 6, 7, 2, 3, 0)
    for i in order:
        greet(m, dest[i])
        greet(m, source[i])

    @pl.when(jnp.logical_not(to_self))
    def _():
        greet(m, dest[1])
        greet(m, source[1])

    for dy, dx in steps:
        greet(chip(dy, dx)[2], d)
    for k in (1, 3, 5, 7):
        greet(fh * 8 + rem(mine + k, 8), d)

    id0, id1 = ids_ref[0:1, :], ids_ref[1:2, :]
    g0, g1 = gate_ref[0:1, :], gate_ref[1:2, :]
    count = id0.shape[1]
    earlier = (iota((count, count), 0) < iota((count, count), 1)).astype(BF16)

    def slots(expert, slot):
        one0, one1 = id0 == expert, id1 == expert
        one = one0 | one1
        before = jnp.dot(one.astype(F32).astype(BF16), earlier, preferred_element_type=F32)
        taken = one & (before.astype(jnp.int32) == slot)
        return taken, one0

    r = iota((128, 1), 0)
    ri, rq, rs = r // 16, rem(r // 4, 4), rem(r, 4)
    expert = jnp.zeros_like(r)
    for i in range(8):
        expert = jnp.where(ri == i, dest[i], expert)
    taken, one0 = slots(expert, rs)
    gate = jnp.sum(jnp.where(taken, jnp.where(one0, g0, g1), 0.0), axis=1, keepdims=True)
    picks = [(taken & (rq == q)).astype(F32).astype(BF16) for q in range(4)]

    def fill(stream, ref, scale):
        total = None
        for q in range(4):
            part = jnp.dot(picks[q], ref[:, q * piece:(q + 1) * piece], preferred_element_type=F32)
            total = part if total is None else total + part
        if scale is not None:
            total = total * scale
        tx[stream] = total.astype(BF16)

    loads[0].wait()
    fill(0, tok, None)
    loads[1].wait()
    fill(1, cot, gate)
    pl.semaphore_wait(barrier, 16 + 7 + 4 - 2 * to_self.astype(jnp.int32))

    waits, guarded = [], []

    def remote(src, dst, send, recv, e=None, dp=None):
        return pltpu.make_async_remote_copy(
            src_ref=src, dst_ref=dst, send_sem=send, recv_sem=recv,
            device_id={"expert": m if e is None else e, "dp": d if dp is None else dp},
            device_id_type=pl.DeviceIdType.MESH,
        )

    def go(copy):
        copy.start()
        waits.append(copy)
        return copy

    def exchange(src, dst, send, recv, dp, is_self):
        copy = remote(src, dst, send, recv, dp=dp)
        if not is_self:
            return go(copy)

        @pl.when(jnp.logical_not(to_self))
        def _():
            copy.start()

        @pl.when(to_self)
        def _():
            pltpu.make_async_copy(src, dst, recv).start()

        guarded.append(copy)
        return copy

    def block(ref, row, size=16):
        return ref.at[pl.ds(row if isinstance(row, int) else pl.multiple_of(row, 16), size)]

    b_copies = {}
    for way, order in ((1, (4, 5, 6, 7)), (0, (2, 3, 0, 1))):
        for stream in range(2):
            for i in order:
                b_copies[stream, i] = exchange(
                    block(tx.at[stream], i * 16), block(packed.at[stream, way, fh], s * 64 + (i % 4) * 16),
                    b_s.at[stream, i], b_r.at[stream, i], dest[i], i == 1)

    weights = []
    for i, ref in enumerate((win, wout)):
        loads[2 + i].wait()
        weights.append(go(remote(ref.at[0], ref.at[1], w_s.at[i], w_r.at[i], e=sibling)))

    def matrix(n, same):
        return same(iota((n, n), 0), iota((n, n), 1)).astype(F32).astype(BF16)

    spread = matrix(256, lambda t, u: (t // 64 == rem(u // 4, 4)) & (rem(t // 4, 16) == u // 16) & (rem(t, 4) == rem(u, 4)))
    swap = matrix(64, lambda t, u: (t // 16 == rem(u // 4, 4)) & (rem(t // 4, 4) == u // 16) & (rem(t, 4) == rem(u, 4)))

    ar = iota((256, 1), 0)
    at, ai, asl = ar // 32, rem(ar // 4, 8), rem(ar, 4)
    aoff = jnp.zeros_like(ar)
    for i, o in enumerate(offsets(at // 2)):
        aoff = jnp.where(ai == i, o, aoff)
    all_taken, _ = slots(rem(xh + rem(at, 2), 2) * NZ + rem(z + aoff, NZ), asl)
    dall[...] = all_taken.astype(F32).astype(BF16)

    for way in range(2):
        for stream in range(2):
            for i in range(4 * way, 4 * way + 4):
                b_copies[stream, i].wait_recv()
            ref = block(packed.at[stream, way, fh], s * 64, 64)
            for k, step in enumerate(steps):
                go(remote(ref, ref, ag_s.at[stream, way, k], ag_r.at[stream, way, fh, s], e=chip(*step)[2]))

    def unpack(stream, way, target):
        for step in reversed(steps):
            ts_, tf, _ = chip(*step)
            ref = block(packed.at[stream, way, tf], ts_ * 64, 64)
            remote(ref, ref, ag_s.at[stream, way, 0], ag_r.at[stream, way, tf, ts_], e=sibling).wait_recv()
        for f in range(2):
            got = jnp.dot(spread, packed[stream, way, f], preferred_element_type=F32).astype(BF16)
            for q in range(4):
                cols = slice(f * half + q * piece, f * half + (q + 1) * piece)
                target[way * 64:(way + 1) * 64, cols] = got[q * 64:(q + 1) * 64]

    chunk = half // 2
    e_copies = []
    for way in range(2):
        rows = slice(way * 64, (way + 1) * 64)
        unpack(0, way, x_ref)
        if way == 0:
            weights[0].wait_recv()
        slopes = []
        for i in range(2):
            preact = None
            for k in range(4):
                cols = slice(k * chunk, (k + 1) * chunk)
                part = jnp.dot(x_ref[rows, cols], win[i, cols, :], preferred_element_type=F32)
                preact = part if preact is None else preact + part
            square = preact * preact
            th = jnp.tanh(K0 * preact * (1.0 + K1 * square))
            hid[i, rows, :] = (0.5 * preact * (1.0 + th)).astype(BF16)
            slopes.append(0.5 * (1.0 + th) + 0.5 * preact * (1.0 - th * th) * (K0 * (1.0 + 3.0 * K1 * square)))
        unpack(1, way, g_ref)
        if way == 0:
            weights[1].wait_recv()
        grads = []
        for i in range(2):
            post = None
            for k in range(4):
                cols = slice(k * chunk, (k + 1) * chunk)
                part = lax.dot_general(g_ref[rows, cols], wout[i, :, cols], NT, preferred_element_type=F32)
                post = part if post is None else post + part
            grads.append((post * slopes[i]).astype(BF16))
        for k in range(4):
            cols = slice(k * chunk, (k + 1) * chunk)
            part = lax.dot_general(grads[0], win[0, cols, :], NT, preferred_element_type=F32)
            part = part + lax.dot_general(grads[1], win[1, cols, :], NT, preferred_element_type=F32)
            here = slice((k % 2) * chunk, (k % 2 + 1) * chunk)
            q_ref[way, k // 2, :, here] = part
            es[way, k // 2, :, here] = part.astype(BF16)
        row = []
        for k, step in enumerate(steps):
            ts_, tf, e = chip(*step)
            row.append(go(remote(
                block(es.at[way, tf], ts_ * 16), er.at[way, k], e_ss.at[way, k], e_rs.at[way, k], e=e)))
        e_copies.append(row)

    g_copy = go(remote(g_ref, g_sib, g_ss, g_rs, e=sibling))
    hid_copy = go(remote(hid.at[1], hid_sib, h_ss, h_rs, e=sibling))

    f_copies = []
    for way in range(2):
        total = q_ref[way, fh, pl.ds(pl.multiple_of(s * 16, 16), 16), :]
        for k in reversed(range(len(steps))):
            e_copies[way][k].wait_recv()
            total = total + er[way, k].astype(F32)
        total = total.astype(BF16)
        stacked = jnp.concatenate([total[:, q * piece:(q + 1) * piece] for q in range(4)], axis=0)
        fs[way] = jnp.dot(swap, stacked, preferred_element_type=F32).astype(BF16)
        f_copies.append([
            exchange(block(fs.at[way], j * 16), block(fr.at[way], j * 16), f_ss.at[way, j], f_rs.at[way, j],
                     source[4 * way + j], way == 0 and j == 1)
            for j in range(4)
        ])

    hid_copy.wait_recv()
    turned = jnp.concatenate([hid[0].astype(F32).T, hid_sib[...].astype(F32).T], axis=1).astype(BF16)
    g_copy.wait_recv()
    for k in range(4):
        cols = slice(k * chunk, (k + 1) * chunk)
        both = jnp.concatenate([g_ref[:, cols], g_sib[:, cols]], axis=0)
        wog[:, cols] = jnp.dot(turned, both, preferred_element_type=F32).astype(BF16)
    store = pltpu.make_async_copy(wog, wog_hbm, ld_sem.at[4])
    store.start()

    t_copies = []
    for way in range(2):
        for copy in f_copies[way]:
            copy.wait_recv()
        got = jnp.dot(swap, fr[way], preferred_element_type=F32).astype(BF16)
        for k in range(8):
            ts[way, k] = got[(k // 2) * 16:(k // 2 + 1) * 16, (k % 2) * 128:(k % 2 + 1) * 128]
        for k in range(1, 8):
            there = rem(mine + k, 8)
            t_copies.append(go(remote(
                ts.at[way, there], block(tr, mine * 32 + way * 16), t_ss.at[way, k], t_rs.at[way, k], e=fh * 8 + there)))
        tr[pl.ds(pl.multiple_of(mine * 32 + way * 16, 16), 16), :] = ts[way, mine]

    for copy in t_copies:
        copy.wait_recv()
    out_ref[...] = lax.dot_general(dall[...], tr[...], TN, preferred_element_type=F32).astype(BF16)

    for copy in waits:
        copy.wait_send()

    @pl.when(jnp.logical_not(to_self))
    def _():
        for copy in guarded:
            copy.wait_send()

    store.wait()


def shards(tokens, cotangent, gate_values, expert_ids, weight_in, weight_out):
    count, width = tokens.shape
    hidden = weight_in.shape[2]
    dma = pltpu.SemaphoreType.DMA
    half = width // 2
    vmem = pl.BlockSpec(memory_space=pltpu.VMEM)
    hbm = pl.BlockSpec(memory_space=pltpu.HBM)
    out, grad = pl.pallas_call(
        kernel,
        out_shape=(
            jax.ShapeDtypeStruct((count, width // PLANE), BF16),
            jax.ShapeDtypeStruct((hidden, width), BF16),
        ),
        in_specs=[hbm, hbm, vmem, vmem, hbm, hbm],
        out_specs=(vmem, hbm),
        scratch_shapes=[
            pltpu.VMEM((count, half), BF16),
            pltpu.VMEM((count, half), BF16),
            pltpu.VMEM((2, width, hidden), BF16),
            pltpu.VMEM((2, hidden, width), BF16),
            pltpu.VMEM((hidden, width), BF16),
            pltpu.VMEM((2, 128, half // 4), BF16),
            pltpu.VMEM((2, 2, 2, 256, half // 4), BF16),
            pltpu.VMEM((128, width), BF16),
            pltpu.VMEM((128, width), BF16),
            pltpu.VMEM((128, width), BF16),
            pltpu.VMEM((2, 128, hidden), BF16),
            pltpu.VMEM((128, hidden), BF16),
            pltpu.VMEM((2, 2, 64, half), BF16),
            pltpu.VMEM((2, 7, 16, half), BF16),
            pltpu.VMEM((2, 2, 64, half), F32),
            pltpu.VMEM((2, 64, half // 4), BF16),
            pltpu.VMEM((2, 64, half // 4), BF16),
            pltpu.VMEM((2, 8, 16, width // PLANE), BF16),
            pltpu.VMEM((256, width // PLANE), BF16),
            pltpu.VMEM((256, count), BF16),
            dma((5,)),
            dma((2, 8)), dma((2, 8)),
            dma((2,)), dma((2,)),
            dma((2, 2, 7)), dma((2, 2, 2, 4)),
            dma, dma,
            dma, dma,
            dma((2, 7)), dma((2, 7)),
            dma((2, 4)), dma((2, 4)),
            dma((2, 8)), dma((2, 8)),
        ],
        compiler_params=pltpu.CompilerParams(
            collective_id=0, has_side_effects=True, vmem_limit_bytes=63 * 1024 * 1024
        ),
    )(tokens, cotangent, expert_ids.T, gate_values.T, weight_in[0], weight_out[0])
    return out, grad[None]


def solution(mesh):
    placed = (
        P("dp", None),
        P("dp", None),
        P("dp", None),
        P("dp", None),
        P("dp", None, "expert"),
        P("dp", "expert", None),
    )
    return jax.shard_map(
        shards,
        mesh=mesh,
        in_specs=placed,
        out_specs=(P("dp", "expert"), P("dp", "expert", None)),
        check_vma=False,
    )
```

time: 407 us -> 87.7 us (0.22)
  the two profiles are of different devices: /device:TPU:27 before, /device:TPU:7 now
where the time goes in v2:
time: 87.7 us; the launch traced here: 87.4 us
  Pallas kernels  83.1 us (95%)
  local copies, waits for them, and re-layouts  3.68 us (4%)
    pallas_call x1, Pallas kernels, shards(): pl.pallas_call(kernel, out_shape=(jax.ShapeDtypeStruct((count, width // P...  83.1 us
    unnamed x2, local copies, waits for them, and re-layouts  3.68 us

profile of v2, /device:TPU:7, one launch (start us, length us, event | category | flops | bytes accessed | tf_op | source)
XLA Modules:
  0.0 87.4 jit_solution(3783041115179363751)
XLA Ops:
  0.6 83.1 %shard_map.77 = (bf16[128,128]{1,0:T(8,128)(2,1)}, bf16[256,2048]{1,0:T(8,128)(2,1)}) custom-call(bf16[128,2048]{1,0:T(8,128)(2,1)} %tok_hbm.1, bf16[128,2048]{1,0:T(8,128)(2,1)} %cot_hbm.1, s32[2,128]{1,0:T(2,128)} %bitcast.8, f32[2,128]{1,0:T(2,128)} %bitcast.9, bf16[2048,256]{1,0:T(8,128)(2,1)} %bitcast.6, bf16[256,2048]{1,0:T(8,128)(2,1)} %bitcast.7), custom_call_target="tpu_custom_call" | custom-call | tf_op jit(solution)/shard_map/pallas_call | solution.py:308
  83.8 1.4 %copy.10 = bf16[128,128]{1,0:T(8,128)(2,1)} copy(bf16[128,128]{1,0:T(8,128)(2,1)} %get-tuple-element.8) | data formatting | bytes 65536
  85.1 2.3 %copy.11 = bf16[1,256,2048]{2,1,0:T(8,128)(2,1)} copy(bf16[1,256,2048]{2,1,0:T(8,128)(2,1)} %bitcast.5) | data formatting | bytes 2097152

commit v3 on v2

--- a/solution.py
+++ b/solution.py
@@ -31,8 +31,8 @@
 
 
 def kernel(
-    tok_hbm, cot_hbm, ids_ref, gate_ref, win_hbm, wout_hbm, out_ref, wog_hbm,
-    tok, cot, win, wout, wog, tx, packed, x_ref, g_ref, g_sib, hid, hid_sib,
+    tok_hbm, cot_hbm, ids_ref, gate_ref, win_hbm, wout_hbm, out_ref, wog,
+    tok, cot, win, wout, tx, packed, x_ref, g_ref, g_sib, hid, hid_sib,
     es, er, q_ref, fs, fr, ts, tr, dall,
     ld_sem, b_s, b_r, w_s, w_r, ag_s, ag_r, g_ss, g_rs, h_ss, h_rs, e_ss, e_rs, f_ss, f_rs, t_ss, t_rs,
 ):
@@ -154,12 +154,15 @@
         return ref.at[pl.ds(row if isinstance(row, int) else pl.multiple_of(row, 16), size)]
 
     b_copies = {}
-    for way, order in ((1, (4, 5, 6, 7)), (0, (2, 3, 0, 1))):
+
+    def send_b(way, order):
         for stream in range(2):
             for i in order:
                 b_copies[stream, i] = exchange(
                     block(tx.at[stream], i * 16), block(packed.at[stream, way, fh], s * 64 + (i % 4) * 16),
                     b_s.at[stream, i], b_r.at[stream, i], dest[i], i == 1)
+
+    send_b(1, (4, 5, 6, 7))
 
     weights = []
     for i, ref in enumerate((win, wout)):
@@ -179,6 +182,8 @@
         aoff = jnp.where(ai == i, o, aoff)
     all_taken, _ = slots(rem(xh + rem(at, 2), 2) * NZ + rem(z + aoff, NZ), asl)
     dall[...] = all_taken.astype(F32).astype(BF16)
+
+    send_b(0, (2, 3, 0, 1))
 
     for way in range(2):
         for stream in range(2):
@@ -267,8 +272,6 @@
         cols = slice(k * chunk, (k + 1) * chunk)
         both = jnp.concatenate([g_ref[:, cols], g_sib[:, cols]], axis=0)
         wog[:, cols] = jnp.dot(turned, both, preferred_element_type=F32).astype(BF16)
-    store = pltpu.make_async_copy(wog, wog_hbm, ld_sem.at[4])
-    store.start()
 
     t_copies = []
     for way in range(2):
@@ -295,8 +298,6 @@
         for copy in guarded:
             copy.wait_send()
 
-    store.wait()
-
 
 def shards(tokens, cotangent, gate_values, expert_ids, weight_in, weight_out):
     count, width = tokens.shape
@@ -308,17 +309,16 @@
     out, grad = pl.pallas_call(
         kernel,
         out_shape=(
-            jax.ShapeDtypeStruct((count, width // PLANE), BF16),
-            jax.ShapeDtypeStruct((hidden, width), BF16),
+            pltpu.VMEM((count, width // PLANE), BF16),
+            pltpu.VMEM((hidden, width), BF16),
         ),
         in_specs=[hbm, hbm, vmem, vmem, hbm, hbm],
-        out_specs=(vmem, hbm),
+        out_specs=(vmem, vmem),
         scratch_shapes=[
             pltpu.VMEM((count, half), BF16),
             pltpu.VMEM((count, half), BF16),
             pltpu.VMEM((2, width, hidden), BF16),
             pltpu.VMEM((2, hidden, width), BF16),
-            pltpu.VMEM((hidden, width), BF16),
             pltpu.VMEM((2, 128, half // 4), BF16),
             pltpu.VMEM((2, 2, 2, 256, half // 4), BF16),
             pltpu.VMEM((128, width), BF16),
@@ -334,7 +334,7 @@
             pltpu.VMEM((2, 8, 16, width // PLANE), BF16),
             pltpu.VMEM((256, width // PLANE), BF16),
             pltpu.VMEM((256, count), BF16),
-            dma((5,)),
+            dma((4,)),
             dma((2, 8)), dma((2, 8)),
             dma((2,)), dma((2,)),
             dma((2, 2, 7)), dma((2, 2, 2, 4)),
@@ -345,7 +345,7 @@
             dma((2, 8)), dma((2, 8)),
         ],
         compiler_params=pltpu.CompilerParams(
-            collective_id=0, has_side_effects=True, vmem_limit_bytes=63 * 1024 * 1024
+            collective_id=0, has_side_effects=True, vmem_limit_bytes=58 * 1024 * 1024
         ),
     )(tokens, cotangent, expert_ids.T, gate_values.T, weight_in[0], weight_out[0])
     return out, grad[None]

time: 87.7 us -> 84.9 us (0.968)
  local copies, waits for them, and re-layouts: 3.68 us -> 1.59 us
    unnamed x2, local copies, waits for them, and re-layouts: 3.68 us -> 1.59 us
where the time goes in v3:
time: 84.9 us; the launch traced here: 84.7 us
  Pallas kernels  82.5 us (97%)
  local copies, waits for them, and re-layouts  1.59 us (2%)
    pallas_call x1, Pallas kernels, shards(): pl.pallas_call(kernel, out_shape=(pltpu.VMEM((count, width // PLANE), BF1...  82.5 us

profile of v3, /device:TPU:7, one launch (start us, length us, event | category | flops | bytes accessed | tf_op | source)
XLA Modules:
  0.0 84.7 jit_solution(9101309362771986234)
XLA Ops:
  0.6 82.5 %shard_map.77 = (bf16[128,128]{1,0:T(8,128)(2,1)S(1)}, bf16[256,2048]{1,0:T(8,128)(2,1)S(1)}) custom-call(bf16[128,2048]{1,0:T(8,128)(2,1)} %tok_hbm.1, bf16[128,2048]{1,0:T(8,128)(2,1)} %cot_hbm.1, s32[2,128]{1,0:T(2,128)} %bitcast.8, f32[2,128]{1,0:T(2,128)} %bitcast.9, bf16[2048,256]{1,0:T(8,128)(2,1)} %bitcast.6, bf16[256,2048]{1,0:T(8,128)(2,1)} %bitcast.7), custom_call_target="tpu_custom_call" | custom-call | tf_op jit(solution)/shard_map/pallas_call | solution.py:309
  83.1 0.6 copy.10
  83.8 1.0 %copy.11 = bf16[1,256,2048]{2,1,0:T(8,128)(2,1)} copy(bf16[1,256,2048]{2,1,0:T(8,128)(2,1)S(1)} %bitcast.5) | data formatting | bytes 2097152

commit v4 on v3

--- a/solution.py
+++ b/solution.py
@@ -62,15 +62,17 @@
         for i, (src, dst) in enumerate(
             ((tok_hbm.at[:, columns], tok), (cot_hbm.at[:, columns], cot), (win_hbm, win.at[0]), (wout_hbm, wout.at[0])))
     ]
+    barrier = pltpu.get_barrier_semaphore()
+
+    def greet(e, dp):
+        pl.semaphore_signal(barrier, inc=1, device_id={"expert": e, "dp": dp}, device_id_type=pl.DeviceIdType.MESH)
+
+    for i in (4, 5, 6, 7):
+        greet(m, dest[i])
+        greet(m, source[i])
     for copy in loads:
         copy.start()
-    barrier = pltpu.get_barrier_semaphore()
-
-    def greet(e, dp):
-        pl.semaphore_signal(barrier, inc=1, device_id={"expert": e, "dp": dp}, device_id_type=pl.DeviceIdType.MESH)
-
-    order = (4, 5, 6, 7, 2, 3, 0)
-    for i in order:
+    for i in (2, 3, 0):
         greet(m, dest[i])
         greet(m, source[i])
 
@@ -206,6 +208,15 @@
 
     chunk = half // 2
     e_copies = []
+
+    def send_e(way):
+        row = []
+        for k, step in enumerate(steps):
+            ts_, tf, e = chip(*step)
+            row.append(go(remote(
+                block(es.at[way, tf], ts_ * 16), er.at[way, k], e_ss.at[way, k], e_rs.at[way, k], e=e)))
+        e_copies.append(row)
+
     for way in range(2):
         rows = slice(way * 64, (way + 1) * 64)
         unpack(0, way, x_ref)
@@ -225,6 +236,8 @@
         unpack(1, way, g_ref)
         if way == 0:
             weights[1].wait_recv()
+        else:
+            send_e(0)
         grads = []
         for i in range(2):
             post = None
@@ -240,12 +253,8 @@
             here = slice((k % 2) * chunk, (k % 2 + 1) * chunk)
             q_ref[way, k // 2, :, here] = part
             es[way, k // 2, :, here] = part.astype(BF16)
-        row = []
-        for k, step in enumerate(steps):
-            ts_, tf, e = chip(*step)
-            row.append(go(remote(
-                block(es.at[way, tf], ts_ * 16), er.at[way, k], e_ss.at[way, k], e_rs.at[way, k], e=e)))
-        e_copies.append(row)
+        if way == 1:
+            send_e(1)
 
     g_copy = go(remote(g_ref, g_sib, g_ss, g_rs, e=sibling))
     hid_copy = go(remote(hid.at[1], hid_sib, h_ss, h_rs, e=sibling))

time: 84.9 us -> 86.9 us (1.024); the launches traced: 84.7 us -> 85.4 us
  no operation moved by 1% of the time
where the time goes in v4:
time: 86.9 us; the launch traced here: 85.4 us
  Pallas kernels  83.2 us (96%)
  local copies, waits for them, and re-layouts  1.59 us (2%)
    pallas_call x1, Pallas kernels, shards(): pl.pallas_call(kernel, out_shape=(pltpu.VMEM((count, width // PLANE), BF1...  83.2 us

profile of v4, /device:TPU:7, one launch (start us, length us, event | category | flops | bytes accessed | tf_op | source)
XLA Modules:
  0.0 85.4 jit_solution(15238588456175550580)
XLA Ops:
  0.6 83.2 %shard_map.77 = (bf16[128,128]{1,0:T(8,128)(2,1)S(1)}, bf16[256,2048]{1,0:T(8,128)(2,1)S(1)}) custom-call(bf16[128,2048]{1,0:T(8,128)(2,1)} %tok_hbm.1, bf16[128,2048]{1,0:T(8,128)(2,1)} %cot_hbm.1, s32[2,128]{1,0:T(2,128)} %bitcast.8, f32[2,128]{1,0:T(2,128)} %bitcast.9, bf16[2048,256]{1,0:T(8,128)(2,1)} %bitcast.6, bf16[256,2048]{1,0:T(8,128)(2,1)} %bitcast.7), custom_call_target="tpu_custom_call" | custom-call | tf_op jit(solution)/shard_map/pallas_call | solution.py:318
  83.8 0.6 copy.10
  84.5 1.0 %copy.11 = bf16[1,256,2048]{2,1,0:T(8,128)(2,1)} copy(bf16[1,256,2048]{2,1,0:T(8,128)(2,1)S(1)} %bitcast.5) | data formatting | bytes 2097152
